TPU v7x, 32 devices: a whole 2x2x4 slice. The times are simulated.
32 devices in a mesh: dp: 2 (over y), expert: 16 (over z, x, core).
Axes of the slice: x: 2, y: 2, z: 4, core: 2. Of those that a mesh axis runs over, the one named last changes fastest.
Arguments:
- tokens: bfloat16 [8192, 1024], P(('dp', 'expert')), may hold values from -6 to 6
- cotangent: bfloat16 [8192, 1024], P(('dp', 'expert')), may hold values from -1.1953125 to 1.1953125
- prob: bfloat16 [8192], P(('dp', 'expert')), may hold values from 0.19921875 to 1
- assign: int32 [8192, 1], P(('dp', 'expert')), may hold values from 0 to 15; in each aligned block of 256 rows (0 to 255, 256 to 511, ...) at most 48 rows name the same one
- w_gate: bfloat16 [16, 1024, 1024], P('expert'), may hold values from -0.1875 to 0.1875
- w_up: bfloat16 [16, 1024, 1024], P('expert'), may hold values from -0.1875 to 0.1875
- w_down: bfloat16 [16, 1024, 1024], P('expert'), may hold values from -0.1875 to 0.1875
Outputs:
- grad_tokens: bfloat16 [8192, 1024], P(('dp', 'expert'))
- grad_prob: bfloat16 [8192], P(('dp', 'expert'))
- grad_gate: float32 [16, 1024, 1024], P('expert', 'dp')
- grad_up: float32 [16, 1024, 1024], P('expert', 'dp')
- grad_down: float32 [16, 1024, 1024], P('expert', 'dp')
Inputs may be any that keep to these rules, and one draw needn't show every extreme that they name: `assign`: among the 256 tokens of one device (aligned blocks of rows), at most 48 are assigned to one expert, and in every draw some expert receives exactly 48 tokens of some device.
All inputs are finite; a program needn't handle non-finite values.
Results may differ from a plain program's by a relative error of at most 0.015.
Values may be sent and summed in bfloat16 or wider, within the bound.
A program may use at most 128 MiB of HBM per device.

v0:
```python
import jax
import jax.numpy as jnp
from jax import lax
from jax.sharding import PartitionSpec as P


def placement_of(assign_dev, experts, capacity):
    chosen = (assign_dev[:, None] == jnp.arange(experts, dtype=jnp.int32)[None, :]).astype(
        jnp.int32
    )
    before = jnp.cumsum(chosen, axis=0) - chosen
    position = jnp.sum(before * chosen, axis=1)
    slot = assign_dev * capacity + position
    return jnp.arange(experts * capacity, dtype=jnp.int32)[:, None] == slot[None, :]


def recompute(rows_in, gate_weight, up_weight, down_weight):
    gate = jnp.dot(rows_in, gate_weight, preferred_element_type=jnp.float32)
    up = jnp.dot(rows_in, up_weight, preferred_element_type=jnp.float32)
    sigmoid_gate = jax.nn.sigmoid(gate)
    activation = gate * sigmoid_gate
    hidden = (activation * up).astype(jnp.bfloat16)
    expert_out = jnp.dot(hidden, down_weight, preferred_element_type=jnp.float32)
    return (gate, up, sigmoid_gate, activation, hidden, expert_out)


def local(tokens, cotangent, prob, assign, w_gate, w_up, w_down):
    experts = lax.axis_size("expert")
    tok_rows = tokens.shape[0]
    width = tokens.shape[1]
    capacity = 3 * tok_rows // experts
    slots_all = experts * capacity
    gate_weight = w_gate[0]
    up_weight = w_up[0]
    down_weight = w_down[0]
    place = placement_of(assign[:, 0], experts, capacity)
    weights = place.astype(jnp.bfloat16)
    send_rows = (
        jnp.dot(weights, tokens, preferred_element_type=jnp.float32)
        .astype(jnp.bfloat16)
        .reshape(experts, capacity, width)
    )
    send_cot = (
        jnp.dot(weights, cotangent, preferred_element_type=jnp.float32)
        .astype(jnp.bfloat16)
        .reshape(experts, capacity, width)
    )
    send_prob = (
        jnp.sum(jnp.where(place, prob[None, :].astype(jnp.float32), 0.0), axis=1)
        .astype(jnp.bfloat16)
        .reshape(experts, capacity)
    )
    recv_rows, recv_cot, recv_prob = (
        lax.all_to_all(send_rows, "expert", split_axis=0, concat_axis=0, tiled=True),
        lax.all_to_all(send_cot, "expert", split_axis=0, concat_axis=0, tiled=True),
        lax.all_to_all(send_prob, "expert", split_axis=0, concat_axis=0, tiled=True),
    )
    rows_in = recv_rows.reshape(slots_all, width)
    gate, up, sigmoid_gate, activation, hidden, expert_out = recompute(
        rows_in, gate_weight, up_weight, down_weight
    )
    cot_in = recv_cot.reshape(slots_all, width)
    prob_in = recv_prob.reshape(slots_all)
    grad_pr = jnp.sum(cot_in.astype(jnp.float32) * expert_out, axis=1).astype(jnp.bfloat16)
    scaled = (prob_in.astype(jnp.float32)[:, None] * cot_in.astype(jnp.float32)).astype(
        jnp.bfloat16
    )
    grad_hidden = lax.dot_general(
        scaled, down_weight, (((1,), (1,)), ((), ())), preferred_element_type=jnp.float32
    )
    grad_gate_pre = (grad_hidden * up * sigmoid_gate * (1.0 + gate * (1.0 - sigmoid_gate))).astype(
        jnp.bfloat16
    )
    grad_up_pre = (grad_hidden * activation).astype(jnp.bfloat16)
    grad_rows = lax.dot_general(
        grad_gate_pre, gate_weight, (((1,), (1,)), ((), ())), preferred_element_type=jnp.float32
    )
    grad_rows = grad_rows + lax.dot_general(
        grad_up_pre, up_weight, (((1,), (1,)), ((), ())), preferred_element_type=jnp.float32
    )
    grad_rows = grad_rows.astype(jnp.bfloat16)
    back_rows, back_prob = (
        lax.all_to_all(
            grad_rows.reshape(experts, capacity, width),
            "expert",
            split_axis=0,
            concat_axis=0,
            tiled=True,
        ),
        lax.all_to_all(
            grad_pr.reshape(experts, capacity), "expert", split_axis=0, concat_axis=0, tiled=True
        ),
    )
    grad_tokens = lax.dot_general(
        weights,
        back_rows.reshape(slots_all, width),
        (((0,), (0,)), ((), ())),
        preferred_element_type=jnp.float32,
    ).astype(jnp.bfloat16)
    grad_prob = jnp.sum(
        jnp.where(place, back_prob.reshape(slots_all)[:, None].astype(jnp.float32), 0.0), axis=0
    ).astype(jnp.bfloat16)
    part_gate = lax.dot_general(
        rows_in, grad_gate_pre, (((0,), (0,)), ((), ())), preferred_element_type=jnp.float32
    )
    part_up = lax.dot_general(
        rows_in, grad_up_pre, (((0,), (0,)), ((), ())), preferred_element_type=jnp.float32
    )
    part_down = lax.dot_general(
        hidden, scaled, (((0,), (0,)), ((), ())), preferred_element_type=jnp.float32
    )
    grad_gate, grad_up, grad_down = (
        lax.psum_scatter(
            part_gate[None].astype(jnp.bfloat16), "dp", scatter_dimension=1, tiled=True
        ).astype(jnp.float32),
        lax.psum_scatter(
            part_up[None].astype(jnp.bfloat16), "dp", scatter_dimension=1, tiled=True
        ).astype(jnp.float32),
        lax.psum_scatter(
            part_down[None].astype(jnp.bfloat16), "dp", scatter_dimension=1, tiled=True
        ).astype(jnp.float32),
    )
    return (grad_tokens, grad_prob, grad_gate, grad_up, grad_down)


def solution(mesh):
    placed = (
        P(("dp", "expert"), None),
        P(("dp", "expert"), None),
        P(("dp", "expert")),
        P(("dp", "expert"), None),
        P("expert", None, None),
        P("expert", None, None),
        P("expert", None, None),
    )
    return jax.shard_map(
        local,
        mesh=mesh,
        in_specs=placed,
        out_specs=(
            P(("dp", "expert"), None),
            P(("dp", "expert")),
            P("expert", "dp", None),
            P("expert", "dp", None),
            P("expert", "dp", None),
        ),
        check_vma=False,
    )
```

profile of v0, /device:TPU:15, one launch (start us, length us, event | category | flops | bytes accessed | tf_op | source)
XLA Modules:
  0.0 234.4 jit_solution(13314787603572554296)
XLA Ops:
  7.2 0.8 fusion.26
  8.8 0.8 fusion.25
  10.3 2.8 %convolution_convert_fusion = bf16[768,1024]{1,0:T(8,128)(2,1)} fusion(bf16[256,1024]{1,0:T(8,128)(2,1)} %param.7, s32[256]{0:T(256)S(1)} %multiply_add_fusion), kind=kOutput, calls=%fused_computation.27 | convolution fusion | flops 403636224 | bytes 2098176 | tf_op jit(solution)/shard_map/dot_general | solution.py:39
  13.0 6.7 %all-to-all-start.2 = ((bf16[16,48,1024]{2,1,0:T(8,128)(2,1)}), bf16[16,48,1024]{2,1,0:T(8,128)(2,1)}, u32[]{:S(2)}, u32[]{:S(2)}) async-start(bf16[16,48,1024]{2,1,0:T(8,128)(2,1)} %bitcast.80), calls=%async_computation.2 | async-start | bytes 3145728 | tf_op jit(solution)/shard_map/all_to_all | solution.py:54
  19.7 1.7 convolution_convert_fusion.1
  21.5 34.6 %all-to-all-done.2 = bf16[16,48,1024]{2,1,0:T(8,128)(2,1)} async-done(((bf16[16,48,1024]{2,1,0:T(8,128)(2,1)}), bf16[16,48,1024]{2,1,0:T(8,128)(2,1)}, u32[]{:S(2)}, u32[]{:S(2)}) %all-to-all-start.2) | async-done | bytes 1572896 | tf_op jit(solution)/shard_map/all_to_all | solution.py:54
  56.0 4.9 %all-to-all-start.1 = ((bf16[16,48,1024]{2,1,0:T(8,128)(2,1)}), bf16[16,48,1024]{2,1,0:T(8,128)(2,1)}, u32[]{:S(2)}, u32[]{:S(2)}) async-start(bf16[16,48,1024]{2,1,0:T(8,128)(2,1)} %bitcast.79), calls=%async_computation.1 | async-start | bytes 3145728 | tf_op jit(solution)/shard_map/all_to_all | solution.py:55
  60.9 3.9 %fusion.6 = f32[768,1024]{1,0:T(8,128)S(1)} fusion(bf16[768,1024]{1,0:T(8,128)(2,1)} %bitcast.8, bf16[1,1024,1024]{2,1,0:T(8,128)(2,1)} %param.11), kind=kOutput, calls=%fused_computation.14 | convolution fusion | flops 1610612736 | bytes 6815744 | tf_op jit(solution)/shard_map/dot_general | solution.py:18
  64.8 1.7 copy-done.4
  66.5 5.6 %multiply_convert_fusion = (bf16[768,1024]{1,0:T(8,128)(2,1)}, f32[768,1024]{1,0:T(8,128)}) fusion(f32[768,1024]{1,0:T(8,128)S(1)} %fusion.6, bf16[768,1024]{1,0:T(8,128)(2,1)} %bitcast.8, bf16[1,1024,1024]{2,1,0:T(8,128)(2,1)S(1)} %copy-done), kind=kOutput, calls=%fused_computation.6 | convolution fusion | flops 1615331328 | bytes 11534336 | tf_op jit(solution)/shard_map/dot_general | solution.py:19
  72.0 25.2 %all-to-all-done.1 = bf16[16,48,1024]{2,1,0:T(8,128)(2,1)} async-done(((bf16[16,48,1024]{2,1,0:T(8,128)(2,1)}), bf16[16,48,1024]{2,1,0:T(8,128)(2,1)}, u32[]{:S(2)}, u32[]{:S(2)}) %all-to-all-start.1) | async-done | bytes 1572896 | tf_op jit(solution)/shard_map/all_to_all | solution.py:55
  97.2 4.4 %fusion.1 = bf16[768]{0:T(1024)(128)(2,1)S(1)} fusion(bf16[16,48,1024]{2,1,0:T(8,128)(2,1)} %all-to-all-done.1, bf16[768,1024]{1,0:T(8,128)(2,1)} %get-tuple-element.9, bf16[1,1024,1024]{2,1,0:T(8,128)(2,1)} %param.13), kind=kOutput, calls=%fused_computation.4 | convolution fusion | flops 1612971264 | bytes 5244416 | tf_op jit(solution)/shard_map/dot_general | solution.py:23
  101.6 0.7 convert_element_type.177
  102.3 4.9 %all-to-all-start.4 = ((bf16[16,1,48]{2,1,0:T(2,128)(2,1)}), bf16[16,1,48]{2,1,0:T(2,128)(2,1)S(1)}, u32[]{:S(2)}, u32[]{:S(2)}) async-start(bf16[16,1,48]{2,1,0:T(2,128)(2,1)} %convert_element_type.177), calls=%async_computation.4 | async-start | bytes 16384 | tf_op jit(solution)/shard_map/all_to_all | solution.py:90
  107.3 3.7 %all-to-all-done.4 = bf16[16,1,48]{2,1,0:T(2,128)(2,1)S(1)} async-done(((bf16[16,1,48]{2,1,0:T(2,128)(2,1)}), bf16[16,1,48]{2,1,0:T(2,128)(2,1)S(1)}, u32[]{:S(2)}, u32[]{:S(2)}) %all-to-all-start.4) | async-done | bytes 1568 | tf_op jit(solution)/shard_map/all_to_all | solution.py:90
  111.0 0.8 select_reduce_fusion
  111.9 9.0 %all_to_all.27 = bf16[16,1,48]{2,1,0:T(2,128)(2,1)S(1)} all-to-all(bf16[16,1,48]{2,1,0:T(2,128)(2,1)S(1)} %convert_element_type.176), channel_id=1, replica_groups=mesh['dp'=2,'expert'=16] {'expert'}, dimensions={0} | all-to-all | bytes 3072 | tf_op jit(solution)/shard_map/all_to_all | solution.py:56
  121.0 1.8 fusion.2
  122.8 3.2 %convert_bitcast_fusion = bf16[1,1024,1024]{2,1,0:T(8,128)(2,1)} fusion(bf16[768,1024]{1,0:T(8,128)(2,1)S(1)} %copy-done.6, bf16[768,1024]{1,0:T(8,128)(2,1)S(1)} %fusion.2), kind=kOutput, calls=%fused_computation.24 | convolution fusion | flops 1611661312 | bytes 5242880 | tf_op jit(solution)/shard_map/dot_general | solution.py:109
  126.3 1.9 fusion
  128.3 6.7 %multiply_convert_fusion.1 = (bf16[768,1024]{1,0:T(8,128)(2,1)}, bf16[768,1024]{1,0:T(8,128)(2,1)S(1)}) fusion(f32[768,1024]{1,0:T(8,128)} %copy-done.4, f32[768,1024]{1,0:T(8,128)} %get-tuple-element.10, bf16[768,1024]{1,0:T(8,128)(2,1)S(1)} %bitcast.81, bf16[1,1024,1024]{2,1,0:T(8,128)(2,1)S(1)} %copy-done.2), kind=kOutput, calls=%fused_computation.8 | convolution fusion | flops 1620836352 | bytes 13107200 | tf_op jit(solution)/shard_map/dot_general | solution.py:68
  135.0 1.1 copy-done.7
  136.2 4.6 %convert_bitcast_fusion.2 = bf16[1,1024,1024]{2,1,0:T(8,128)(2,1)} fusion(bf16[768,1024]{1,0:T(8,128)(2,1)} %bitcast.8, bf16[768,1024]{1,0:T(8,128)(2,1)S(1)} %get-tuple-element.8), kind=kOutput, calls=%fused_computation.26 | convolution fusion | flops 1611661312 | bytes 5242880 | tf_op jit(solution)/shard_map/dot_general | solution.py:103
  140.9 5.1 %convert_bitcast_fusion.1 = bf16[1,1024,1024]{2,1,0:T(8,128)(2,1)} fusion(bf16[768,1024]{1,0:T(8,128)(2,1)} %bitcast.8, bf16[768,1024]{1,0:T(8,128)(2,1)} %get-tuple-element.7), kind=kOutput, calls=%fused_computation.25 | convolution fusion | flops 1611661312 | bytes 5242880 | tf_op jit(solution)/shard_map/dot_general | solution.py:106
  146.0 4.0 %fusion.4 = f32[768,1024]{1,0:T(8,128)S(1)} fusion(bf16[768,1024]{1,0:T(8,128)(2,1)} %copy-done.7, bf16[1,1024,1024]{2,1,0:T(8,128)(2,1)} %param.11), kind=kOutput, calls=%fused_computation.12 | convolution fusion | flops 1610612736 | bytes 6815744 | tf_op jit(solution)/shard_map/dot_general | solution.py:75
  150.0 1.8 add_convert_fusion
  151.8 42.1 %all_to_all.28 = bf16[16,48,1024]{2,1,0:T(8,128)(2,1)S(1)} all-to-all(bf16[16,48,1024]{2,1,0:T(8,128)(2,1)S(1)} %bitcast.82), channel_id=1, replica_groups=mesh['dp'=2,'expert'=16] {'expert'}, dimensions={0} | all-to-all | bytes 3145728 | tf_op jit(solution)/shard_map/all_to_all | solution.py:83
  193.9 1.4 convolution_convert_fusion.2
  195.4 2.8 %convert_element_type.171 = f32[1,512,1024]{2,1,0:T(8,128)} convert(bf16[1,512,1024]{2,1,0:T(8,128)(2,1)} %reduce-scatter.8.cloned.1.call-done) | non-fusion elementwise | flops 524288 | bytes 3145728 | tf_op jit(solution)/shard_map/convert_element_type | solution.py:121
  198.1 2.8 %convert_element_type.162 = f32[1,512,1024]{2,1,0:T(8,128)} convert(bf16[1,512,1024]{2,1,0:T(8,128)(2,1)} %reduce-scatter.4.cloned.1.call-done) | non-fusion elementwise | flops 524288 | bytes 3145728 | tf_op jit(solution)/shard_map/convert_element_type | solution.py:115
  200.9 24.2 %reduce-scatter.6.cloned.1.call-done = bf16[1,512,1024]{2,1,0:T(8,128)(2,1)} async-done(((bf16[1,1024,1024]{2,1,0:T(8,128)(2,1)}), bf16[1,512,1024]{2,1,0:T(8,128)(2,1)}) %reduce-scatter.6.cloned.1.call-update) | async-done | bytes 1048592 | tf_op jit(solution)/shard_map/reduce_scatter | solution.py:116
  225.1 2.8 %convert_element_type.165 = f32[1,512,1024]{2,1,0:T(8,128)} convert(bf16[1,512,1024]{2,1,0:T(8,128)(2,1)} %reduce-scatter.6.cloned.1.call-done) | non-fusion elementwise | flops 524288 | bytes 3145728 | tf_op jit(solution)/shard_map/convert_element_type | solution.py:118
  (34 shorter events, 2.3 us)
Async XLA Ops:
  7.2 59.3 %copy-start = (bf16[1,1024,1024]{2,1,0:T(8,128)(2,1)S(1)}, bf16[1,1024,1024]{2,1,0:T(8,128)(2,1)}, u32[]{:S(2)}) copy-start(bf16[1,1024,1024]{2,1,0:T(8,128)(2,1)} %param.12) | copy-start | bytes 6291460
  13.0 6.7 %copy-start.1 = (bf16[256,1024]{1,0:T(8,128)(2,1)S(1)}, bf16[256,1024]{1,0:T(8,128)(2,1)}, u32[]{:S(2)}) copy-start(bf16[256,1024]{1,0:T(8,128)(2,1)} %param.8) | copy-start | bytes 1572868
  13.0 43.0 %all-to-all-start.2 = ((bf16[16,48,1024]{2,1,0:T(8,128)(2,1)}), bf16[16,48,1024]{2,1,0:T(8,128)(2,1)}, u32[]{:S(2)}, u32[]{:S(2)}) async-start(bf16[16,48,1024]{2,1,0:T(8,128)(2,1)} %bitcast.80), calls=%async_computation.2 | async-start | bytes 3145728 | tf_op jit(solution)/shard_map/all_to_all | solution.py:54
  56.0 41.2 %all-to-all-start.1 = ((bf16[16,48,1024]{2,1,0:T(8,128)(2,1)}), bf16[16,48,1024]{2,1,0:T(8,128)(2,1)}, u32[]{:S(2)}, u32[]{:S(2)}) async-start(bf16[16,48,1024]{2,1,0:T(8,128)(2,1)} %bitcast.79), calls=%async_computation.1 | async-start | bytes 3145728 | tf_op jit(solution)/shard_map/all_to_all | solution.py:55
  64.8 1.7 copy-start.4
  97.2 10.1 %copy-start.3 = (bf16[256]{0:T(256)(128)(2,1)S(1)}, bf16[256]{0:T(256)(128)(2,1)}, u32[]{:S(2)}) copy-start(bf16[256]{0:T(256)(128)(2,1)} %param.9) | copy-start | bytes 1540
  102.3 8.6 %all-to-all-start.4 = ((bf16[16,1,48]{2,1,0:T(2,128)(2,1)}), bf16[16,1,48]{2,1,0:T(2,128)(2,1)S(1)}, u32[]{:S(2)}, u32[]{:S(2)}) async-start(bf16[16,1,48]{2,1,0:T(2,128)(2,1)} %convert_element_type.177), calls=%async_computation.4 | async-start | bytes 16384 | tf_op jit(solution)/shard_map/all_to_all | solution.py:90
  107.2 88.1 %reduce-scatter.8.cloned.1.call-start = ((), (), s32[]{:S(2)}) async-start(), calls=%async_computation.10 | async-start | bytes 3145728 | tf_op jit(solution)/shard_map/reduce_scatter | solution.py:119
  121.0 1.9 copy-start.6
  126.0 72.1 %reduce-scatter.4.cloned.1.call-start = ((), (), s32[]{:S(2)}) async-start(), calls=%async_computation.8 | async-start | bytes 3145728 | tf_op jit(solution)/shard_map/reduce_scatter | solution.py:113
  126.3 2.1 copy-start.2
  135.0 1.1 copy-start.7
  140.8 84.3 %reduce-scatter.6.cloned.1.call-start = ((), (), s32[]{:S(2)}) async-start(), calls=%async_computation.9 | async-start | bytes 3145728 | tf_op jit(solution)/shard_map/reduce_scatter | solution.py:116
  145.9 4.0 %copy-start.5 = (bf16[768,1024]{1,0:T(8,128)(2,1)S(1)}, bf16[768,1024]{1,0:T(8,128)(2,1)}, u32[]{:S(2)}) copy-start(bf16[768,1024]{1,0:T(8,128)(2,1)} %get-tuple-element.7) | copy-start | bytes 4718596
Sparse Core Ops, SparseCore 0:
  126.2 29.9 reduce-scatter.7
  159.1 31.8 reduce-scatter.3
  193.2 31.8 reduce-scatter.5
where the time goes:
time: 238 us; the launch traced here: 234 us
  waiting for transfers between devices  87.6 us (37%)
  blocking collectives  51.1 us (21%)
  matrix products  45.1 us (19%)
  starting transfers between devices  16.8 us (7%)
  other arithmetic  15.8 us (7%)
  between operations  13.9 us (6%)
  local copies, waits for them, and re-layouts  4.14 us (2%)
    all_to_all x1, blocking collectives, local(): lax.all_to_all(grad_rows.reshape(experts, capacity, width), 'expert', spl...  42.1 us
    all_to_all x1, waiting for transfers between devices, local(): lax.all_to_all(send_rows, 'expert', split_axis=0, concat_axis=0, tiled=True)  34.6 us
    all_to_all x1, waiting for transfers between devices, local(): lax.all_to_all(send_cot, 'expert', split_axis=0, concat_axis=0, tiled=True)  25.2 us
    reduce_scatter x1, waiting for transfers between devices, local(): lax.psum_scatter(part_up[None].astype(jnp.bfloat16), 'dp', scatter_dimens...  24.2 us
    all_to_all x1, blocking collectives, local(): lax.all_to_all(send_prob, 'expert', split_axis=0, concat_axis=0, tiled=True)  8.97 us
    convert_element_type x3, other arithmetic, local(): grad_gate, grad_up, grad_down = (lax.psum_scatter(part_gate[None].astype(...  8.37 us
    all_to_all x1, starting transfers between devices, local(): lax.all_to_all(send_rows, 'expert', split_axis=0, concat_axis=0, tiled=True)  6.69 us
    dot_general x1, matrix products, local(): lax.dot_general(scaled, down_weight, (((1,), (1,)), ((), ())), preferred_...  6.68 us
  transfers between devices with their start and end apart: 6, of which 4 were waited for; matrix products, arithmetic and copies ran while one was open for 18% of the time, Pallas kernels for 0%

commit v1 on v0

v1 whole, which is shorter than its diff:
```python
import functools
import math

import jax
import jax.numpy as jnp
from jax import lax
from jax.experimental import pallas as pl
from jax.experimental.pallas import tpu as pltpu
from jax.sharding import PartitionSpec as P

MESH = pl.DeviceIdType.MESH
F32 = jnp.float32
BF16 = jnp.bfloat16
BLOCK_ORDER = (2, 3, 1, 0)
BLOCKS = 4


def tn(a, b):
    return lax.dot_general(a, b, (((0,), (0,)), ((), ())), preferred_element_type=F32)


def nt(a, b):
    return lax.dot_general(a, b, (((1,), (1,)), ((), ())), preferred_element_type=F32)


def nn(a, b):
    return jnp.dot(a, b, preferred_element_type=F32)


def kernel(
    n, ndp, cap,
    tok, cot, prob, assign, wg_hbm, wu_hbm, wd_hbm,
    gt_out, gp_out, gg_out, gu_out, gd_out,
    wg, wu, wd, st, ss, rt, rs, hid, ggp, gup, acc, bs, br, ps, pr,
    w_sem, st_s, st_r, ss_s, ss_r, ft_s, ft_r, fs_s, fs_r, b_s, b_r, p_s, p_r, o_sem,
):
    k = lax.axis_index("dp")
    me = lax.axis_index("expert")
    own_tokens, width = tok.shape
    ff = wg.shape[1]
    per = n // BLOCKS
    rows = per * cap
    half = acc.shape[1]
    my_block, my_place = me // per, lax.rem(me, per)

    def block_of(c):
        high = lax.rem(my_block // 2 + c // 2, 2)
        low = lax.rem(lax.rem(my_block, 2) + c % 2, 2)
        return high * 2 + low

    def partner(c, j):
        return block_of(c) * per + lax.rem(my_place + j, per)

    def slot_rows(s):
        return pl.ds(pl.multiple_of(s * cap, 16), cap)

    def block_rows(b):
        return pl.ds(pl.multiple_of(b * rows, 16), rows)

    barrier = pltpu.get_barrier_semaphore()
    for c in range(BLOCKS):
        for j in range(per):
            if c or j:
                pl.semaphore_signal(
                    barrier, inc=1, device_id=(k, partner(c, j)), device_id_type=MESH
                )
    for j in range(1, ndp):
        pl.semaphore_signal(
            barrier, inc=1, device_id=(lax.rem(k + j, ndp), me), device_id_type=MESH
        )

    weights = [
        pltpu.make_async_copy(src, dst, w_sem.at[i])
        for i, (src, dst) in enumerate(((wg_hbm, wg), (wu_hbm, wu), (wd_hbm, wd)))
    ]
    for copy in weights:
        copy.start()

    expert = lax.broadcasted_iota(jnp.int32, (n, own_tokens), 0)
    chosen = (expert == assign[...]).astype(F32)
    earlier = (
        lax.broadcasted_iota(jnp.int32, (own_tokens, own_tokens), 0)
        < lax.broadcasted_iota(jnp.int32, (own_tokens, own_tokens), 1)
    ).astype(F32)
    before = nn(chosen.astype(BF16), earlier.astype(BF16))
    slot = jnp.sum(chosen * (before + expert.astype(F32) * cap), axis=0, keepdims=True)
    slot = slot.astype(jnp.int32)
    prob_row = prob[...].astype(F32)

    def place(b):
        return lax.broadcasted_iota(jnp.int32, (rows, own_tokens), 0) + b * rows == slot

    def to_slot(src, dst, s, send, recv, c, j):
        return pltpu.make_async_remote_copy(
            src_ref=src,
            dst_ref=dst,
            send_sem=send.at[c * per + j],
            recv_sem=recv.at[me],
            device_id=(k, s),
            device_id_type=MESH,
        )

    def out_tok(c, j):
        s = partner(c, j)
        return to_slot(st.at[slot_rows(s)], rt.at[k, slot_rows(me)], s, st_s, st_r, c, j)

    def out_cot(c, j):
        s = partner(c, j)
        return to_slot(ss.at[slot_rows(s)], rs.at[k, slot_rows(me)], s, ss_s, ss_r, c, j)

    def back_grad(c, j):
        s = partner(c, j)
        return to_slot(bs.at[slot_rows(s)], br.at[slot_rows(me)], s, b_s, b_r, c, j)

    def back_prob(c, j):
        s = partner(c, j)
        return to_slot(ps.at[s], pr.at[me], s, p_s, p_r, c, j)

    def arrived(buf, s, recv):
        pltpu.make_async_remote_copy(
            src_ref=buf, dst_ref=buf, send_sem=st_s.at[0], recv_sem=recv.at[s],
            device_id=(k, s), device_id_type=MESH,
        ).wait_recv()

    for step, c in enumerate(BLOCK_ORDER):
        b = block_of(c)
        here = place(b)
        st[block_rows(b), :] = nn(here.astype(F32).astype(BF16), tok[...]).astype(BF16)
        if step == 0:
            pl.semaphore_wait(barrier, n - 1 + ndp - 1)
        for j in range(per):
            if c or j:
                out_tok(c, j).start()
        ss[block_rows(b), :] = nn(
            jnp.where(here, prob_row, 0.0).astype(BF16), cot[...]
        ).astype(BF16)
        for j in range(per):
            if c or j:
                out_cot(c, j).start()
    rt[k, slot_rows(me), :] = st[slot_rows(me), :]
    rs[k, slot_rows(me), :] = ss[slot_rows(me), :]

    def forward(buf, b, j, send, recv):
        view = buf.at[k, block_rows(b)]
        return pltpu.make_async_remote_copy(
            src_ref=view,
            dst_ref=view,
            send_sem=send.at[(j - 1) * BLOCKS + b],
            recv_sem=recv.at[k * BLOCKS + b],
            device_id=(lax.rem(k + j, ndp), me),
            device_id_type=MESH,
        )

    tile = min(512, ff)

    def hidden_grads(g, b):
        here = block_rows(b)

        def body(i, total):
            cols = pl.ds(pl.multiple_of(i * tile, tile), tile)
            x = rt[g, here, :]
            gate = nn(x, wg[:, cols])
            up = nn(x, wu[:, cols])
            grad = nt(rs[g, here, :], wd[cols, :])
            s = jax.nn.sigmoid(gate)
            act = gate * s
            h = (act * up).astype(BF16)
            hid[here, cols] = h
            ggp[here, cols] = (grad * up * s * (1.0 + gate * (1.0 - s))).astype(BF16)
            gup[here, cols] = (grad * act).astype(BF16)
            return total + jnp.sum(grad * h.astype(F32), axis=1, keepdims=True)

        return lax.fori_loop(0, ff // tile, body, jnp.zeros((rows, 1), F32))

    diagonal = lax.broadcasted_iota(jnp.int32, (per, cap, 128), 1) == lax.broadcasted_iota(
        jnp.int32, (per, cap, 128), 2
    )

    def own_block(c):
        b = block_of(c)
        here = block_rows(b)
        dots = hidden_grads(k, b)

        def body(i, carry):
            cols = pl.ds(pl.multiple_of(i * tile, tile), tile)
            grad = nt(ggp[here, :], wg[cols, :]) + nt(gup[here, :], wu[cols, :])
            bs[here, cols] = grad.astype(BF16)
            return carry

        lax.fori_loop(0, width // tile, body, 0)
        line = jnp.sum(jnp.where(diagonal, dots.reshape(per, cap, 1), 0.0), axis=1, keepdims=True)
        ps[pl.ds(b * per, per)] = jnp.broadcast_to(line, (per, 8, 128))
        for j in range(per):
            if c or j:
                back_grad(c, j).start()
                back_prob(c, j).start()
        if c == 0:
            br[slot_rows(me), :] = bs[slot_rows(me), :]
            pr[me] = ps[me]

    for c in BLOCK_ORDER:
        b = block_of(c)
        for j in range(per):
            if c or j:
                s = partner(c, j)
                arrived(rt.at[k, slot_rows(s)], s, st_r)
        for j in range(1, ndp):
            forward(rt, b, j, ft_s, ft_r).start()
        for j in range(per):
            if c or j:
                s = partner(c, j)
                arrived(rs.at[k, slot_rows(s)], s, ss_r)
        for j in range(1, ndp):
            forward(rs, b, j, fs_s, fs_r).start()
        if c == BLOCK_ORDER[0]:
            for copy in weights:
                copy.wait()
        own_block(c)

    mt = math.gcd(256, half)

    def weight_grads(g, first):
        def body(i, carry):
            out = pl.ds(pl.multiple_of(i * mt, mt), mt)
            src = pl.ds(pl.multiple_of(k * half + i * mt, mt), mt)
            x = rt[g, :, src]
            terms = (tn(x, ggp[...]), tn(x, gup[...]), tn(hid[:, src], rs[g]))
            for m in range(3):
                if first:
                    acc[m, out, :] = terms[m]
                else:
                    acc[m, out, :] += terms[m]
            return carry

        lax.fori_loop(0, half // mt, body, 0)

    weight_grads(k, True)

    def peer(j, carry):
        g = lax.rem(k + j, ndp)
        for c in BLOCK_ORDER:
            b = block_of(c)
            for buf, recv in ((rt, ft_r), (rs, fs_r)):
                view = buf.at[g, block_rows(b)]
                pltpu.make_async_remote_copy(
                    src_ref=view, dst_ref=view, send_sem=ft_s.at[0],
                    recv_sem=recv.at[g * BLOCKS + b],
                    device_id=(g, me), device_id_type=MESH,
                ).wait_recv()
            hidden_grads(g, b)
        weight_grads(g, False)
        return carry

    lax.fori_loop(1, ndp, peer, 0)
    outs = [
        pltpu.make_async_copy(acc.at[m], dst, o_sem.at[m])
        for m, dst in enumerate((gg_out, gu_out, gd_out))
    ]
    for copy in outs:
        copy.start()

    total = jnp.zeros((1, own_tokens), F32)
    grads = jnp.zeros((own_tokens, width), F32)
    for c in reversed(BLOCK_ORDER):
        b = block_of(c)
        for j in range(per):
            if c or j:
                s = partner(c, j)
                arrived(br.at[slot_rows(s)], s, b_r)
                arrived(pr.at[s], s, p_r)
        here = place(b).astype(F32)
        grads = grads + tn(here.astype(BF16), br[block_rows(b), :])
        line = pr[pl.ds(b * per, per)][:, 0:1, :]
        column = jnp.sum(jnp.where(diagonal, line, 0.0), axis=2, keepdims=True)
        total = total + jnp.sum(here * column.reshape(rows, 1), axis=0, keepdims=True)
    gt_out[...] = grads.astype(BF16)
    gp_out[...] = (total / prob_row).astype(BF16)

    for c in BLOCK_ORDER:
        for j in range(per):
            if c or j:
                for make in (out_tok, out_cot, back_grad, back_prob):
                    make(c, j).wait_send()
        for j in range(1, ndp):
            forward(rt, block_of(c), j, ft_s, ft_r).wait_send()
            forward(rs, block_of(c), j, fs_s, fs_r).wait_send()
    for copy in outs:
        copy.wait()


def local(n, ndp, tokens, cotangent, prob, assign, w_gate, w_up, w_down):
    own_tokens, width = tokens.shape
    ff = w_gate.shape[2]
    cap = -(-(3 * own_tokens // n) // 16) * 16
    slots = n * cap
    vmem, anywhere = pl.BlockSpec(memory_space=pltpu.VMEM), pl.BlockSpec(memory_space=pl.ANY)
    dma = pltpu.SemaphoreType.DMA
    shape = jax.ShapeDtypeStruct
    grad_tokens, grad_prob, grad_gate, grad_up, grad_down = pl.pallas_call(
        functools.partial(kernel, n, ndp, cap),
        out_shape=(
            shape((own_tokens, width), BF16),
            shape((1, own_tokens), BF16),
            shape((width // ndp, ff), F32),
            shape((width // ndp, ff), F32),
            shape((ff // ndp, width), F32),
        ),
        in_specs=[vmem] * 4 + [anywhere] * 3,
        out_specs=(vmem, vmem, anywhere, anywhere, anywhere),
        scratch_shapes=[
            pltpu.VMEM((width, ff), BF16),
            pltpu.VMEM((width, ff), BF16),
            pltpu.VMEM((ff, width), BF16),
            pltpu.VMEM((slots, width), BF16),
            pltpu.VMEM((slots, width), BF16),
            pltpu.VMEM((ndp, slots, width), BF16),
            pltpu.VMEM((ndp, slots, width), BF16),
            pltpu.VMEM((slots, ff), BF16),
            pltpu.VMEM((slots, ff), BF16),
            pltpu.VMEM((slots, ff), BF16),
            pltpu.VMEM((3, width // ndp, ff), F32),
            pltpu.VMEM((slots, width), BF16),
            pltpu.VMEM((slots, width), BF16),
            pltpu.VMEM((n, 8, 128), F32),
            pltpu.VMEM((n, 8, 128), F32),
            dma((3,)),
            dma((n,)), dma((n,)), dma((n,)), dma((n,)),
            dma((ndp * BLOCKS,)), dma((ndp * BLOCKS,)),
            dma((ndp * BLOCKS,)), dma((ndp * BLOCKS,)),
            dma((n,)), dma((n,)), dma((n,)), dma((n,)),
            dma((3,)),
        ],
        compiler_params=pltpu.CompilerParams(
            collective_id=0, has_side_effects=True, vmem_limit_bytes=62 * 2**20
        ),
        cost_estimate=pl.CostEstimate(
            flops=22 * slots * width * ff, bytes_accessed=16 * width * ff, transcendentals=0
        ),
    )(
        tokens, cotangent, prob.reshape(1, own_tokens), assign.reshape(1, own_tokens),
        w_gate[0], w_up[0], w_down[0],
    )
    return (
        grad_tokens, grad_prob.reshape(own_tokens),
        grad_gate[None], grad_up[None], grad_down[None],
    )


def solution(mesh):
    placed = (
        P(("dp", "expert"), None),
        P(("dp", "expert"), None),
        P(("dp", "expert")),
        P(("dp", "expert"), None),
        P("expert", None, None),
        P("expert", None, None),
        P("expert", None, None),
    )
    return jax.shard_map(
        functools.partial(local, mesh.shape["expert"], mesh.shape["dp"]),
        mesh=mesh,
        in_specs=placed,
        out_specs=(
            P(("dp", "expert"), None),
            P(("dp", "expert")),
            P("expert", "dp", None),
            P("expert", "dp", None),
            P("expert", "dp", None),
        ),
        check_vma=False,
    )
```

time: 238 us -> 159 us (0.67)
  Pallas kernels: 0 us -> 145 us
  waiting for transfers between devices: 87.6 us -> 0 us
  blocking collectives: 51.1 us -> 0 us
  matrix products: 45.1 us -> 0 us
  starting transfers between devices: 16.8 us -> 0 us
  other arithmetic: 15.8 us -> 1.19 us
  between operations: 13.9 us -> 0.64 us
  local copies, waits for them, and re-layouts: 4.14 us -> 10.1 us
    pallas_call x0 -> x1, Pallas kernels: none -> 145 us  [local(): pl.pallas_call(functools.partial(kernel, n, ndp, cap), out_shape=(shape((...]
    all_to_all x3 -> x0, waiting for transfers between devices: 63.4 us -> none  [the longest x1 34.6 us: local(): lax.all_to_all(send_rows, 'expert', split_axis=0, concat_axis=0, tiled=True)]
    all_to_all x2 -> x0, blocking collectives: 51.1 us -> none  [the longest x1 42.1 us: local(): lax.all_to_all(grad_rows.reshape(experts, capacity, width), 'expert', spl...]
    dot_general x12 -> x0, matrix products: 45.1 us -> none  [the longest x1 6.68 us: local(): lax.dot_general(scaled, down_weight, (((1,), (1,)), ((), ())), preferred_...]
    reduce_scatter x3 -> x0, waiting for transfers between devices: 24.2 us -> none  [the longest x1 24.2 us: local(): lax.psum_scatter(part_up[None].astype(jnp.bfloat16), 'dp', scatter_dimens...]
    all_to_all x3 -> x0, starting transfers between devices: 16.5 us -> none  [the longest x1 6.69 us: local(): lax.all_to_all(send_rows, 'expert', split_axis=0, concat_axis=0, tiled=True)]
    convert_element_type x10 -> x0, other arithmetic: 13 us -> none  [the longest x3 8.37 us: local(): grad_gate, grad_up, grad_down = (lax.psum_scatter(part_gate[None].astype(...]
    unnamed x16 -> x8, local copies, waits for them, and re-layouts: 3.02 us -> 8.84 us
  transfers between devices with their start and end apart: 6 -> 0, of which waited for: 4 -> 0; matrix products, arithmetic and copies ran while one was open for 18% -> 0% of each run, Pallas kernels for 0% -> 0%
where the time goes in v1:
time: 159 us; the launch traced here: 157 us
  Pallas kernels  145 us (91%)
  local copies, waits for them, and re-layouts  10.1 us (6%)
    pallas_call x1, Pallas kernels, local(): pl.pallas_call(functools.partial(kernel, n, ndp, cap), out_shape=(shape((...  145 us
    unnamed x8, local copies, waits for them, and re-layouts  8.84 us

profile of v1, /device:TPU:15, one launch (start us, length us, event | category | flops | bytes accessed | tf_op | source)
XLA Modules:
  0.0 157.3 jit_solution(7215015361185721985)
XLA Ops:
  0.6 1.2 reshape.19.prob
  1.9 145.4 %shard_map.110 = (bf16[256,1024]{1,0:T(8,128)(2,1)}, bf16[1,256]{1,0:T(2,128)(2,1)}, f32[512,1024]{1,0:T(8,128)}, f32[512,1024]{1,0:T(8,128)}, f32[512,1024]{1,0:T(8,128)}) custom-call(bf16[256,1024]{1,0:T(8,128)(2,1)} %tok.1, bf16[256,1024]{1,0:T(8,128)(2,1)} %cot.1, bf16[1,256]{1,0:T(2,128)(2,1)} %reshape.19.prob, s32[1,256]{1,0:T(1,128)} %bitcast.13, ...), custom_call_target="tpu_custom_call" | custom-call | flops 17716740096 | bytes 16777216 | tf_op jit(solution)/shard_map/pallas_call | solution.py:299
  147.2 1.2 reduce
  148.4 1.9 %copy.16 = bf16[256,1024]{1,0:T(8,128)(2,1)} copy(bf16[256,1024]{1,0:T(8,128)(2,1)} %get-tuple-element.20) | data formatting | bytes 1048576
  150.3 0.0 copy-start.1
  150.3 3.3 %copy.17 = f32[1,512,1024]{2,1,0:T(8,128)} copy(f32[1,512,1024]{2,1,0:T(8,128)} %bitcast.9) | data formatting | bytes 4194304
  153.6 0.0 copy-done.1
  153.6 0.0 copy-start
  153.6 1.3 copy.18
  154.9 1.0 copy-done
  156.0 1.3 copy.19
Async XLA Ops:
  150.3 3.3 %copy-start.1 = (f32[512,1024]{1,0:T(8,128)S(1)}, f32[512,1024]{1,0:T(8,128)}, u32[]{:S(2)}) copy-start(f32[512,1024]{1,0:T(8,128)} %get-tuple-element.13) | copy-start | bytes 6291460
  153.6 2.3 %copy-start = (f32[512,1024]{1,0:T(8,128)S(1)}, f32[512,1024]{1,0:T(8,128)}, u32[]{:S(2)}) copy-start(f32[512,1024]{1,0:T(8,128)} %get-tuple-element.14) | copy-start | bytes 6291460

commit v2 on v1

--- a/solution.py
+++ b/solution.py
@@ -11,7 +11,7 @@
 MESH = pl.DeviceIdType.MESH
 F32 = jnp.float32
 BF16 = jnp.bfloat16
-BLOCK_ORDER = (2, 3, 1, 0)
+BLOCK_ORDER = (0, 2, 1, 3)
 BLOCKS = 4
 
 
@@ -85,7 +85,7 @@
     before = nn(chosen.astype(BF16), earlier.astype(BF16))
     slot = jnp.sum(chosen * (before + expert.astype(F32) * cap), axis=0, keepdims=True)
     slot = slot.astype(jnp.int32)
-    prob_row = prob[...].astype(F32)
+    prob_row = prob[...].astype(F32).reshape(1, own_tokens)
 
     def place(b):
         return lax.broadcasted_iota(jnp.int32, (rows, own_tokens), 0) + b * rows == slot
@@ -165,9 +165,9 @@
             s = jax.nn.sigmoid(gate)
             act = gate * s
             h = (act * up).astype(BF16)
-            hid[here, cols] = h
-            ggp[here, cols] = (grad * up * s * (1.0 + gate * (1.0 - s))).astype(BF16)
-            gup[here, cols] = (grad * act).astype(BF16)
+            hid[:, cols] = h
+            ggp[:, cols] = (grad * up * s * (1.0 + gate * (1.0 - s))).astype(BF16)
+            gup[:, cols] = (grad * act).astype(BF16)
             return total + jnp.sum(grad * h.astype(F32), axis=1, keepdims=True)
 
         return lax.fori_loop(0, ff // tile, body, jnp.zeros((rows, 1), F32))
@@ -183,7 +183,7 @@
 
         def body(i, carry):
             cols = pl.ds(pl.multiple_of(i * tile, tile), tile)
-            grad = nt(ggp[here, :], wg[cols, :]) + nt(gup[here, :], wu[cols, :])
+            grad = nt(ggp[...], wg[cols, :]) + nt(gup[...], wu[cols, :])
             bs[here, cols] = grad.astype(BF16)
             return carry
 
@@ -198,33 +198,16 @@
             br[slot_rows(me), :] = bs[slot_rows(me), :]
             pr[me] = ps[me]
 
-    for c in BLOCK_ORDER:
-        b = block_of(c)
-        for j in range(per):
-            if c or j:
-                s = partner(c, j)
-                arrived(rt.at[k, slot_rows(s)], s, st_r)
-        for j in range(1, ndp):
-            forward(rt, b, j, ft_s, ft_r).start()
-        for j in range(per):
-            if c or j:
-                s = partner(c, j)
-                arrived(rs.at[k, slot_rows(s)], s, ss_r)
-        for j in range(1, ndp):
-            forward(rs, b, j, fs_s, fs_r).start()
-        if c == BLOCK_ORDER[0]:
-            for copy in weights:
-                copy.wait()
-        own_block(c)
-
     mt = math.gcd(256, half)
 
-    def weight_grads(g, first):
+    def weight_grads(g, b, first):
+        here = block_rows(b)
+
         def body(i, carry):
             out = pl.ds(pl.multiple_of(i * mt, mt), mt)
             src = pl.ds(pl.multiple_of(k * half + i * mt, mt), mt)
-            x = rt[g, :, src]
-            terms = (tn(x, ggp[...]), tn(x, gup[...]), tn(hid[:, src], rs[g]))
+            x = rt[g, here, src]
+            terms = (tn(x, ggp[...]), tn(x, gup[...]), tn(hid[:, src], rs[g, here, :]))
             for m in range(3):
                 if first:
                     acc[m, out, :] = terms[m]
@@ -234,12 +217,11 @@
 
         lax.fori_loop(0, half // mt, body, 0)
 
-    weight_grads(k, True)
-
-    def peer(j, carry):
-        g = lax.rem(k + j, ndp)
-        for c in BLOCK_ORDER:
-            b = block_of(c)
+    def peers_block(c):
+        b = block_of(c)
+
+        def body(j, carry):
+            g = lax.rem(k + j, ndp)
             for buf, recv in ((rt, ft_r), (rs, fs_r)):
                 view = buf.at[g, block_rows(b)]
                 pltpu.make_async_remote_copy(
@@ -248,10 +230,33 @@
                     device_id=(g, me), device_id_type=MESH,
                 ).wait_recv()
             hidden_grads(g, b)
-        weight_grads(g, False)
-        return carry
-
-    lax.fori_loop(1, ndp, peer, 0)
+            weight_grads(g, b, False)
+            return carry
+
+        lax.fori_loop(1, ndp, body, 0)
+
+    for step, c in enumerate(BLOCK_ORDER):
+        b = block_of(c)
+        for j in range(per):
+            if c or j:
+                s = partner(c, j)
+                arrived(rt.at[k, slot_rows(s)], s, st_r)
+        for j in range(1, ndp):
+            forward(rt, b, j, ft_s, ft_r).start()
+        for j in range(per):
+            if c or j:
+                s = partner(c, j)
+                arrived(rs.at[k, slot_rows(s)], s, ss_r)
+        for j in range(1, ndp):
+            forward(rs, b, j, fs_s, fs_r).start()
+        if step == 0:
+            for copy in weights:
+                copy.wait()
+        own_block(c)
+        weight_grads(k, b, step == 0)
+        if step:
+            peers_block(BLOCK_ORDER[step - 1])
+    peers_block(BLOCK_ORDER[-1])
     outs = [
         pltpu.make_async_copy(acc.at[m], dst, o_sem.at[m])
         for m, dst in enumerate((gg_out, gu_out, gd_out))
@@ -261,7 +266,7 @@
 
     total = jnp.zeros((1, own_tokens), F32)
     grads = jnp.zeros((own_tokens, width), F32)
-    for c in reversed(BLOCK_ORDER):
+    for c in BLOCK_ORDER:
         b = block_of(c)
         for j in range(per):
             if c or j:
@@ -286,6 +291,26 @@
             forward(rs, block_of(c), j, fs_s, fs_r).wait_send()
     for copy in outs:
         copy.wait()
+
+
+def hand_on(*refs):
+    for src, dst in zip(refs[: len(refs) // 2], refs[len(refs) // 2 :]):
+        dst[...] = src[...]
+
+
+def handed_on(*arrays):
+    steps = 4
+    blocks = [
+        pl.BlockSpec((a.shape[0] // steps, a.shape[1]), lambda i: (i, 0)) for a in arrays
+    ]
+    return pl.pallas_call(
+        hand_on,
+        grid=(steps,),
+        out_shape=tuple(jax.ShapeDtypeStruct(a.shape, a.dtype) for a in arrays),
+        in_specs=blocks,
+        out_specs=tuple(blocks),
+        compiler_params=pltpu.CompilerParams(vmem_limit_bytes=62 * 2**20),
+    )(*arrays)
 
 
 def local(n, ndp, tokens, cotangent, prob, assign, w_gate, w_up, w_down):
@@ -315,9 +340,9 @@
             pltpu.VMEM((slots, width), BF16),
             pltpu.VMEM((ndp, slots, width), BF16),
             pltpu.VMEM((ndp, slots, width), BF16),
-            pltpu.VMEM((slots, ff), BF16),
-            pltpu.VMEM((slots, ff), BF16),
-            pltpu.VMEM((slots, ff), BF16),
+            pltpu.VMEM((slots // BLOCKS, ff), BF16),
+            pltpu.VMEM((slots // BLOCKS, ff), BF16),
+            pltpu.VMEM((slots // BLOCKS, ff), BF16),
             pltpu.VMEM((3, width // ndp, ff), F32),
             pltpu.VMEM((slots, width), BF16),
             pltpu.VMEM((slots, width), BF16),
@@ -337,8 +362,11 @@
             flops=22 * slots * width * ff, bytes_accessed=16 * width * ff, transcendentals=0
         ),
     )(
-        tokens, cotangent, prob.reshape(1, own_tokens), assign.reshape(1, own_tokens),
+        tokens, cotangent, prob, assign.reshape(1, own_tokens),
         w_gate[0], w_up[0], w_down[0],
+    )
+    grad_tokens, grad_gate, grad_up, grad_down = handed_on(
+        grad_tokens, grad_gate, grad_up, grad_down
     )
     return (
         grad_tokens, grad_prob.reshape(own_tokens),

time: 159 us -> 120 us (0.75); the launches traced: 157 us -> 120 us
  Pallas kernels: 145 us -> 119 us
  local copies, waits for them, and re-layouts: 10.1 us -> 0.01 us
    pallas_call x1, Pallas kernels: 145 us -> 113 us  [local(): pl.pallas_call(functools.partial(kernel, n, ndp, cap), out_shape=(shape((...]
    unnamed x8 -> x2, local copies, waits for them, and re-layouts: 8.84 us -> 0.01 us
    pallas_call x0 -> x1, Pallas kernels: none -> 6.12 us  [handed_on(): pl.pallas_call(hand_on, grid=(steps,), out_shape=tuple((jax.ShapeDtypeStr...]
where the time goes in v2:
time: 120 us
  Pallas kernels  119 us (99%)
    pallas_call x1, Pallas kernels, local(): pl.pallas_call(functools.partial(kernel, n, ndp, cap), out_shape=(shape((...  113 us
    pallas_call x1, Pallas kernels, handed_on(): pl.pallas_call(hand_on, grid=(steps,), out_shape=tuple((jax.ShapeDtypeStr...  6.12 us

profile of v2, /device:TPU:15, one launch (start us, length us, event | category | flops | bytes accessed | tf_op | source)
XLA Modules:
  0.0 120.0 jit_solution(14505675881911699276)
XLA Ops:
  0.6 112.7 %shard_map.110 = (bf16[256,1024]{1,0:T(8,128)(2,1)}, bf16[1,256]{1,0:T(2,128)(2,1)}, f32[512,1024]{1,0:T(8,128)}, f32[512,1024]{1,0:T(8,128)}, f32[512,1024]{1,0:T(8,128)}) custom-call(bf16[256,1024]{1,0:T(8,128)(2,1)} %tok.1, bf16[256,1024]{1,0:T(8,128)(2,1)} %cot.1, bf16[256]{0:T(256)(128)(2,1)} %prob.1, s32[1,256]{1,0:T(1,128)} %bitcast.13, ...), custom_call_target="tpu_custom_call" | custom-call | flops 17716740096 | bytes 16777216 | tf_op jit(solution)/shard_map/pallas_call | solution.py:324
  113.4 0.0 copy-start
  113.4 6.1 %shard_map.111 = (bf16[256,1024]{1,0:T(8,128)(2,1)}, f32[512,1024]{1,0:T(8,128)}, f32[512,1024]{1,0:T(8,128)}, f32[512,1024]{1,0:T(8,128)}) custom-call(bf16[256,1024]{1,0:T(8,128)(2,1)} %get-tuple-element.14.refs_0_, f32[512,1024]{1,0:T(8,128)} %get-tuple-element.15.refs_1_, f32[512,1024]{1,0:T(8,128)} %get-tuple-element.16.refs_2_, ...), custom_call_target="tpu_custom_call" | custom-call | tf_op jit(solution)/shard_map/pallas_call | solution.py:306
  119.5 0.0 copy-done
  119.5 0.5 reduce
Async XLA Ops:
  113.4 6.1 %copy-start = (bf16[1,256]{1,0:T(2,128)(2,1)S(1)}, bf16[1,256]{1,0:T(2,128)(2,1)}, u32[]{:S(2)}) copy-start(bf16[1,256]{1,0:T(2,128)(2,1)} %get-tuple-element.19) | copy-start | bytes 1540

commit v3 on v2

--- a/solution.py
+++ b/solution.py
@@ -31,7 +31,7 @@
     n, ndp, cap,
     tok, cot, prob, assign, wg_hbm, wu_hbm, wd_hbm,
     gt_out, gp_out, gg_out, gu_out, gd_out,
-    wg, wu, wd, st, ss, rt, rs, hid, ggp, gup, acc, bs, br, ps, pr,
+    wg, wu, wd, st, ss, rt, rs, hid, ggp, gup, acc, acc16, mine, bs, br, ps, pr,
     w_sem, st_s, st_r, ss_s, ss_r, ft_s, ft_r, fs_s, fs_r, b_s, b_r, p_s, p_r, o_sem,
 ):
     k = lax.axis_index("dp")
@@ -235,6 +235,23 @@
 
         lax.fori_loop(1, ndp, body, 0)
 
+    def in_order(c, first):
+        b = block_of(c)
+        for j in range(per):
+            if c or j:
+                s = partner(c, j)
+                arrived(br.at[slot_rows(s)], s, b_r)
+                arrived(pr.at[s], s, p_r)
+        here = place(b).astype(F32)
+        grads = tn(here.astype(BF16), br[block_rows(b), :])
+        if first:
+            mine[...] = grads
+        else:
+            mine[...] += grads
+        line = pr[pl.ds(b * per, per)][:, 0:1, :]
+        column = jnp.sum(jnp.where(diagonal, line, 0.0), axis=2, keepdims=True)
+        return jnp.sum(here * column.reshape(rows, 1), axis=0, keepdims=True)
+
     for step, c in enumerate(BLOCK_ORDER):
         b = block_of(c)
         for j in range(per):
@@ -256,29 +273,18 @@
         weight_grads(k, b, step == 0)
         if step:
             peers_block(BLOCK_ORDER[step - 1])
+    total = in_order(BLOCK_ORDER[0], True)
+    for c in BLOCK_ORDER[1:-1]:
+        total = total + in_order(c, False)
     peers_block(BLOCK_ORDER[-1])
-    outs = [
-        pltpu.make_async_copy(acc.at[m], dst, o_sem.at[m])
-        for m, dst in enumerate((gg_out, gu_out, gd_out))
-    ]
-    for copy in outs:
-        copy.start()
-
-    total = jnp.zeros((1, own_tokens), F32)
-    grads = jnp.zeros((own_tokens, width), F32)
-    for c in BLOCK_ORDER:
-        b = block_of(c)
-        for j in range(per):
-            if c or j:
-                s = partner(c, j)
-                arrived(br.at[slot_rows(s)], s, b_r)
-                arrived(pr.at[s], s, p_r)
-        here = place(b).astype(F32)
-        grads = grads + tn(here.astype(BF16), br[block_rows(b), :])
-        line = pr[pl.ds(b * per, per)][:, 0:1, :]
-        column = jnp.sum(jnp.where(diagonal, line, 0.0), axis=2, keepdims=True)
-        total = total + jnp.sum(here * column.reshape(rows, 1), axis=0, keepdims=True)
-    gt_out[...] = grads.astype(BF16)
+    outs = []
+    for m, dst in enumerate((gg_out, gu_out, gd_out)):
+        acc16[m] = acc[m].astype(BF16)
+        outs.append(pltpu.make_async_copy(acc16.at[m], dst, o_sem.at[m]))
+        outs[m].start()
+
+    total = total + in_order(BLOCK_ORDER[-1], False)
+    gt_out[...] = mine[...].astype(BF16)
     gp_out[...] = (total / prob_row).astype(BF16)
 
     for c in BLOCK_ORDER:
@@ -295,18 +301,18 @@
 
 def hand_on(*refs):
     for src, dst in zip(refs[: len(refs) // 2], refs[len(refs) // 2 :]):
-        dst[...] = src[...]
-
-
-def handed_on(*arrays):
-    steps = 4
+        dst[...] = src[...].astype(dst.dtype)
+
+
+def handed_on(arrays, types):
+    steps = 8
     blocks = [
         pl.BlockSpec((a.shape[0] // steps, a.shape[1]), lambda i: (i, 0)) for a in arrays
     ]
     return pl.pallas_call(
         hand_on,
         grid=(steps,),
-        out_shape=tuple(jax.ShapeDtypeStruct(a.shape, a.dtype) for a in arrays),
+        out_shape=tuple(jax.ShapeDtypeStruct(a.shape, t) for a, t in zip(arrays, types)),
         in_specs=blocks,
         out_specs=tuple(blocks),
         compiler_params=pltpu.CompilerParams(vmem_limit_bytes=62 * 2**20),
@@ -326,9 +332,9 @@
         out_shape=(
             shape((own_tokens, width), BF16),
             shape((1, own_tokens), BF16),
-            shape((width // ndp, ff), F32),
-            shape((width // ndp, ff), F32),
-            shape((ff // ndp, width), F32),
+            shape((width // ndp, ff), BF16),
+            shape((width // ndp, ff), BF16),
+            shape((ff // ndp, width), BF16),
         ),
         in_specs=[vmem] * 4 + [anywhere] * 3,
         out_specs=(vmem, vmem, anywhere, anywhere, anywhere),
@@ -344,6 +350,8 @@
             pltpu.VMEM((slots // BLOCKS, ff), BF16),
             pltpu.VMEM((slots // BLOCKS, ff), BF16),
             pltpu.VMEM((3, width // ndp, ff), F32),
+            pltpu.VMEM((3, width // ndp, ff), BF16),
+            pltpu.VMEM((own_tokens, width), F32),
             pltpu.VMEM((slots, width), BF16),
             pltpu.VMEM((slots, width), BF16),
             pltpu.VMEM((n, 8, 128), F32),
@@ -366,7 +374,7 @@
         w_gate[0], w_up[0], w_down[0],
     )
     grad_tokens, grad_gate, grad_up, grad_down = handed_on(
-        grad_tokens, grad_gate, grad_up, grad_down
+        (grad_tokens, grad_gate, grad_up, grad_down), (BF16, F32, F32, F32)
     )
     return (
         grad_tokens, grad_prob.reshape(own_tokens),

time: 120 us -> 122 us (1.017)
  no operation moved by 1% of the time
where the time goes in v3:
time: 122 us
  Pallas kernels  120 us (98%)
    pallas_call x1, Pallas kernels, local(): pl.pallas_call(functools.partial(kernel, n, ndp, cap), out_shape=(shape((...  113 us
    pallas_call x1, Pallas kernels, handed_on(): pl.pallas_call(hand_on, grid=(steps,), out_shape=tuple((jax.ShapeDtypeStr...  7.18 us

profile of v3, /device:TPU:15, one launch (start us, length us, event | category | flops | bytes accessed | tf_op | source)
XLA Modules:
  0.0 121.7 jit_solution(13807893741953300613)
XLA Ops:
  0.6 112.7 %shard_map.110 = (bf16[256,1024]{1,0:T(8,128)(2,1)}, bf16[1,256]{1,0:T(2,128)(2,1)}, bf16[512,1024]{1,0:T(8,128)(2,1)}, bf16[512,1024]{1,0:T(8,128)(2,1)}, bf16[512,1024]{1,0:T(8,128)(2,1)}) custom-call(bf16[256,1024]{1,0:T(8,128)(2,1)} %tok.1, bf16[256,1024]{1,0:T(8,128)(2,1)} %cot.1, bf16[256]{0:T(256)(128)(2,1)} %prob.1, s32[1,256]{1,0:T(1,128)} %bitcast.13, ...), custom_call_target="tpu_custom_call" | custom-call | flops 17716740096 | bytes 16777216 | tf_op jit(solution)/shard_map/pallas_call | solution.py:330
  113.4 1.2 reduce
  114.6 7.2 %shard_map.111 = (bf16[256,1024]{1,0:T(8,128)(2,1)}, f32[512,1024]{1,0:T(8,128)}, f32[512,1024]{1,0:T(8,128)}, f32[512,1024]{1,0:T(8,128)}) custom-call(bf16[256,1024]{1,0:T(8,128)(2,1)} %get-tuple-element.14.refs_0_, bf16[512,1024]{1,0:T(8,128)(2,1)} %get-tuple-element.15.refs_1_, bf16[512,1024]{1,0:T(8,128)(2,1)} %get-tuple-element.16.refs_2_, ...), custom_call_target="tpu_custom_call" | custom-call | tf_op jit(solution)/shard_map/pallas_call | solution.py:312
